TPU v7x, 512 devices: a whole 4x4x16 slice. The times are simulated.
512 devices in a mesh: users: 32 (over y, x, core), items: 16 (over z).
Axes of the slice: x: 4, y: 4, z: 16, core: 2. Of those that a mesh axis runs over, the one named last changes fastest.
Arguments:
- user_emb: bfloat16 [65536, 256], P('users'), may hold values from -0.375 to 0.375
- samples: int32 [512, 64], P('users'), may hold values from 0 to 127, as said below
- pos_item: int32 [65536], P('users'), may hold values from 0 to 16383
- item_feat: bfloat16 [16384, 1024], P(('items', 'users')), may hold values from -0.1875 to 0.1875
- tower_w: bfloat16 [1024, 256], replicated, may hold values from -5 to 5
- item_bias: bfloat16 [16384], P(('items', 'users')), may hold values from -4 to 352
Outputs:
- user_loss: float32 [65536], P('users')
- user_grad: float32 [65536, 256], P(('users', 'items'))
- weight_grad: float32 [1024, 256], replicated
Inputs may be any that keep to these rules, and one draw needn't show every extreme that they name: `samples`: each row lists 64 distinct cluster ids. Clusters k * 8 to (k + 1) * 8 - 1 form item shard k; at most 8 ids of one row fall in any one shard, and in every row some shard holds exactly 8 of them.
All inputs are finite; a program needn't handle non-finite values.
Results may differ from a plain program's by a relative error of at most 0.0036.
Values may be sent and summed in bfloat16 or wider, within the bound.
No kernel may reach another device: no remote copies, remote signals or barrier semaphores. Data moves between devices by JAX's collectives and lax.ppermute only.
A program may use at most 64 MiB of HBM per device.

v0:
```python
import jax
import jax.numpy as jnp
from jax import lax
from jax.sharding import PartitionSpec as P

CL = 128
BU = 128
PEAK = 8
NEG_FILL = -1e30


def body(user_emb, samples, pos_item, item_feat, tower_w, item_bias):
    shard_index = lax.axis_index("items")
    group_size = lax.axis_size("users")
    shard_rows = item_feat.shape[0] * group_size
    shard_clus = shard_rows // CL
    slot_count = min(PEAK, shard_clus)
    shard_feats, bias_rows = (
        lax.all_gather(item_feat, "users", axis=0, tiled=True),
        lax.all_gather(item_bias, "users", axis=0, tiled=True),
    )
    item_rows = jnp.dot(shard_feats, tower_w, preferred_element_type=jnp.float32).astype(
        jnp.bfloat16
    )
    emb_width = item_rows.shape[1]
    emb_tiles = item_rows.reshape(shard_clus, CL, emb_width)
    bias_float = bias_rows.astype(jnp.float32)
    bias_tiles = bias_float.reshape(shard_clus, CL)
    blocks = samples.shape[0]
    step_count = blocks // 4
    local_ids = samples - shard_index * shard_clus
    inside = (local_ids >= 0) & (local_ids < shard_clus)
    rank_in = jnp.cumsum(inside.astype(jnp.int32), axis=1) - 1
    slot_range = jnp.arange(slot_count, dtype=jnp.int32)
    matched = inside[:, None, :] & (rank_in[:, None, :] == slot_range[None, :, None])
    slot_ids = jnp.sum(jnp.where(matched, local_ids[:, None, :], 0), axis=2)
    slot_live = jnp.any(matched, axis=2)
    pos_local = pos_item - shard_index * shard_rows
    pos_live = (pos_local >= 0) & (pos_local < shard_rows)
    pos_index = jnp.clip(pos_local, 0, shard_rows - 1)
    pos_rows = item_rows[pos_index]
    pos_logit = (
        jnp.einsum("ud,ud->u", user_emb, pos_rows, preferred_element_type=jnp.float32)
        + bias_float[pos_index]
    )
    user_steps = user_emb.reshape(step_count, 4, BU, emb_width)
    slot_steps = slot_ids.reshape(step_count, 4, slot_count)
    live_steps = slot_live.reshape(step_count, 4, slot_count)
    pos_steps = pos_logit.reshape(step_count, 4, BU)
    plive_steps = pos_live.reshape(step_count, 4, BU)

    def scores_of(user_rows, cluster_ids, live_ids):
        picked = emb_tiles[cluster_ids]
        raw_scores = jnp.einsum(
            "gud,gkcd->gukc", user_rows, picked, preferred_element_type=jnp.float32
        )
        raw_scores = raw_scores + bias_tiles[cluster_ids][:, None]
        live_mask = jnp.broadcast_to(live_ids[:, None, :, None], raw_scores.shape)
        return (picked, jnp.where(live_mask, raw_scores, NEG_FILL), live_mask)

    def forward(inputs):
        user_rows, cluster_ids, live_ids, pos_part, pos_flag = inputs
        picked, raw_scores, live_mask = scores_of(user_rows, cluster_ids, live_ids)
        row_peak = jnp.maximum(
            jnp.max(raw_scores, axis=(2, 3)), jnp.where(pos_flag, pos_part, NEG_FILL)
        )
        exp_total = jnp.sum(
            jnp.where(live_mask, jnp.exp(raw_scores - row_peak[..., None, None]), 0.0), axis=(2, 3)
        )
        exp_total = exp_total + jnp.where(pos_flag, jnp.exp(pos_part - row_peak), 0.0)
        return (row_peak, exp_total)

    local_peak, local_total = lax.map(
        forward, (user_steps, slot_steps, live_steps, pos_steps, plive_steps)
    )
    local_peak = local_peak.reshape(-1)
    local_total = local_total.reshape(-1)
    pos_value = jnp.where(pos_live, pos_logit, 0.0)
    row_peak = lax.pmax(local_peak, "items")
    exp_total, pos_score = lax.psum(
        (local_total * jnp.exp(local_peak - row_peak), pos_value), "items"
    )
    log_total = row_peak + jnp.log(exp_total)
    user_loss = log_total - pos_score
    pos_weight = jnp.where(pos_live, jnp.exp(pos_logit - log_total) - 1.0, 0.0)

    def weights_of(user_rows, cluster_ids, live_ids, log_part):
        picked, raw_scores, live_mask = scores_of(user_rows, cluster_ids, live_ids)
        soft_weight = jnp.where(
            live_mask, jnp.exp(raw_scores - log_part[..., None, None]), 0.0
        ).astype(jnp.bfloat16)
        return (picked, soft_weight)

    def add_tiles(grad_tiles, user_rows, cluster_ids, live_ids, soft_weight):
        contrib = jnp.einsum(
            "gukc,gud->gkcd", soft_weight, user_rows, preferred_element_type=jnp.float32
        )
        contrib = jnp.where(live_ids[..., None, None], contrib, 0.0)
        return grad_tiles.at[cluster_ids.reshape(-1)].add(contrib.reshape(-1, CL, emb_width))

    def backward_both(grad_tiles, inputs):
        user_rows, cluster_ids, live_ids, log_part = inputs
        picked, soft_weight = weights_of(user_rows, cluster_ids, live_ids, log_part)
        grad_users = jnp.einsum(
            "gukc,gkcd->gud", soft_weight, picked, preferred_element_type=jnp.float32
        )
        return (add_tiles(grad_tiles, user_rows, cluster_ids, live_ids, soft_weight), grad_users)

    start_tiles = jnp.zeros((shard_clus, CL, emb_width), jnp.float32)
    scan_inputs = (user_steps, slot_steps, live_steps, log_total.reshape(step_count, 4, BU))
    pos_terms = pos_weight[:, None] * pos_rows.astype(jnp.float32)
    grad_tiles, grad_users = lax.scan(backward_both, start_tiles, scan_inputs)
    grad_users = grad_users.reshape(-1, emb_width) + pos_terms
    user_grad = lax.psum_scatter(grad_users, "items", scatter_dimension=0, tiled=True)
    grad_items = (
        grad_tiles.reshape(shard_rows, emb_width)
        .at[pos_index]
        .add(pos_weight[:, None] * user_emb.astype(jnp.float32))
    )
    contract = (((0,), (0,)), ((), ()))
    part_weight = lax.dot_general(
        shard_feats.astype(jnp.float32), grad_items, contract, precision=lax.Precision.HIGHEST
    )
    weight_grad = lax.psum(part_weight, ("users", "items"))
    return (user_loss, user_grad, weight_grad)


def solution(mesh):
    return jax.shard_map(
        body,
        mesh=mesh,
        in_specs=(
            P("users", None),
            P("users", None),
            P("users"),
            P(("items", "users"), None),
            P(),
            P(("items", "users")),
        ),
        out_specs=(P("users"), P(("users", "items"), None), P()),
        check_vma=False,
    )
```

profile of v0, /device:TPU:4, one launch (start us, length us, event | category | flops | bytes accessed | tf_op | source)
XLA Modules:
  0.0 829.6 jit_solution(18017372859213118122)
XLA Ops:
  11.7 58.1 %all-reduce = bf16[1024]{0:T(1024)(128)(2,1)S(1)} all-reduce(bf16[1024]{0:T(1024)(128)(2,1)S(1)} %dynamic-update-slice), channel_id=1, replica_groups=mesh['users'=32,'items'=16] {'users'}, use_global_device_ids=true, to_apply=%add | all-reduce | flops 1024 | bytes 4096
  70.5 8.6 %gather_fusion.5 = f32[2048]{0:T(1024)S(1)} fusion(f32[1024]{0:T(1024)S(1)} %get-tuple-element.174, s32[2048]{0:T(1024)S(1)} %get-tuple-element.164), kind=kCustom, calls=%fused_computation.5 | custom fusion | bytes 24576 | tf_op jit(solution)/shard_map/gather | solution.py:44
  79.9 2.3 convolution_convert_fusion
  82.2 7.5 gather_fusion.4
  90.7 17.9 %while.24 = (s32[]{:T(128)}, f32[4,4,128]{2,1,0:T(4,128)S(1)}, f32[4,4,128]{2,1,0:T(4,128)S(1)}, pred[4,4,8]{2,1,0:T(4,128)(4,1)S(1)}, bf16[4,4,128,256]{3,2,1,0...) while((s32[]{:T(128)}, f32[4,4,128]{2,1,0:T(4,128)S(1)}, ...), condition=%wide.region_6.7_spmd, body=%wide.region_3.6_spmd.sunk | while | flops 272633440 | bytes 15036589 | solution.py:73
  92.1 1.9 fusion.43
  96.5 1.9 fusion.43
  108.6 36.2 %pmax.7 = f32[2048]{0:T(1024)S(1)} all-reduce(f32[2048]{0:T(1024)S(1)} %bitcast.148), channel_id=1, replica_groups=mesh['users'=32,'items'=16] {'items'}, use_global_device_ids=true, to_apply=%region_7.8 | all-reduce | flops 2048 | bytes 16384 | tf_op jit(solution)/shard_map/pmax | solution.py:79
  144.7 52.7 %all-reduce.1 = (f32[2048]{0:T(1024)S(1)}, f32[2048]{0:T(1024)S(1)}) all-reduce(f32[2048]{0:T(1024)S(1)} %exponential_multiply_fusion, f32[2048]{0:T(1024)S(1)} %get-tuple-element.161), channel_id=1, replica_groups=mesh['users'=32,'items'=16] {'items'}, use_global_device_ids=true, to_apply=%region_8.9 | all-reduce | flops 4096 | bytes 32768 | tf_op jit(solution)/shard_map/psum | solution.py:80
  197.5 64.0 %while.25 = (s32[]{:T(128)}, f32[8,128,256]{2,1,0:T(8,128)S(1)}, f32[4,4,128,256]{3,2,1,0:T(8,128)}, s32[4,4,8]{2,1,0:T(4,128)S(1)}, pred[4,4,8]{2,1,0:T(4,128)(...) while((s32[]{:T(128)}, f32[8,128,256]{2,1,0:T(8,128)S(1)}, ...), condition=%wide.region_12.13_spmd, body=%wide.region_10.12_spmd.sunk | while | flops 810026176 | bytes 42005372 | solution.py:112
  198.3 2.0 gather_fusion.2
  200.4 2.6 select_convert_fusion.2
  204.3 2.8 convolution_select_fusion.2
  207.1 6.4 scatter_fusion
  214.3 2.0 gather_fusion.2
  216.4 2.6 select_convert_fusion.2
  220.3 2.8 convolution_select_fusion.2
  223.1 6.5 scatter_fusion
  230.4 2.0 gather_fusion.2
  232.4 2.6 select_convert_fusion.2
  236.3 2.8 convolution_select_fusion.2
  239.1 6.5 scatter_fusion
  246.3 2.0 gather_fusion.2
  248.4 2.6 select_convert_fusion.2
  252.3 2.8 convolution_select_fusion.2
  255.1 6.5 scatter_fusion
  261.5 15.9 %scatter_custom_fusion.1 = f32[1024,256]{1,0:T(8,128)S(1)} fusion(f32[1024,256]{1,0:T(8,128)S(1)} %bitcast.128, s32[2048]{0:T(1024)S(1)} %get-tuple-element.165, bf16[2048,256]{1,0:T(8,128)(2,1)} %bitcast.137, f32[2048]{0:T(1024)S(1)} %get-tuple-element.159), kind=kCustom, calls=%fused_computation.46 | custom fusion | flops 1572864 | bytes 2105344 | tf_op jit(solution)/shard_map/scatter-add | solution.py:118
  277.4 4.5 convolution_bitcast_fusion.1
  282.0 3.3 fusion.17
  286.0 462.6 %all-reduce.4.cloned.1.call-done = f32[1024,256]{0,1:T(8,128)} async-done(((f32[1024,256]{0,1:T(8,128)}), f32[1024,256]{0,1:T(8,128)}) %all-reduce.4.cloned.1.call-update) | async-done | bytes 1048592 | tf_op jit(solution)/shard_map/psum | solution.py:124
  748.6 2.5 copy.14
  751.1 72.0 %reduce-scatter.2.cloned.1.call-done = f32[128,256]{1,0:T(8,128)} async-done(((f32[2048,256]{1,0:T(8,128)}), f32[128,256]{1,0:T(8,128)}) %reduce-scatter.2.cloned.1.call-update) | async-done | bytes 131088 | tf_op jit(solution)/shard_map/reduce_scatter | solution.py:114
  (134 shorter events, 29.3 us)
Async XLA Ops:
  7.2 72.7 %copy-start = (bf16[1024,256]{1,0:T(8,128)(2,1)S(1)}, bf16[1024,256]{1,0:T(8,128)(2,1)}, u32[]{:S(2)}) copy-start(bf16[1024,256]{1,0:T(8,128)(2,1)} %param.14) | copy-start | bytes 1572868
  7.2 72.7 %all-gather.2.cloned.1.call-start = ((), (), s32[]{:S(2)}) async-start(), calls=%async_computation.1 | async-start | bytes 2162688 | tf_op jit(solution)/shard_map/all_gather | solution.py:19
  7.9 740.7 %all-reduce.4.cloned.1.call-start = ((), (), s32[]{:S(2)}) async-start(), calls=%async_computation.3 | async-start | bytes 2097152 | tf_op jit(solution)/shard_map/psum | solution.py:124
  82.2 7.5 copy-start.2
  89.7 1.0 copy-start.5
  89.7 0.7 copy-start.7
  93.9 1.2 copy-start.3
  98.4 1.2 copy-start.3
  102.9 1.2 copy-start.3
  107.3 1.2 copy-start.3
  198.3 2.0 copy-start.4
  200.4 2.6 copy-start.1
  214.3 2.0 copy-start.4
  216.4 2.6 copy-start.1
  230.4 2.0 copy-start.4
  232.4 2.6 copy-start.1
  246.3 2.0 copy-start.4
  248.4 2.6 copy-start.1
  277.4 4.6 copy-start.6
  282.0 541.1 %reduce-scatter.2.cloned.1.call-start = ((), (), s32[]{:S(2)}) async-start(), calls=%async_computation.2 | async-start | bytes 2228224 | tf_op jit(solution)/shard_map/reduce_scatter | solution.py:114
Sparse Core Ops, SparseCore 0:
  11.1 63.0 all-gather.1
  282.1 466.4 all-reduce.3
  752.0 71.0 reduce-scatter.1
where the time goes:
time: 831 us; the launch traced here: 830 us
  waiting for transfers between devices  535 us (64%)
  blocking collectives  147 us (18%)
  other arithmetic  51.7 us (6%)
  matrix products  40.9 us (5%)
  local copies, waits for them, and re-layouts  39.6 us (5%)
  between operations  14.6 us (2%)
    psum x1, waiting for transfers between devices, body(): weight_grad = lax.psum(part_weight, ('users', 'items'))  463 us
    reduce_scatter x1, waiting for transfers between devices, body(): lax.psum_scatter(grad_users, 'items', scatter_dimension=0, tiled=True)  72 us
    unnamed x1, blocking collectives  58.1 us
    psum x1, blocking collectives, body(): lax.psum((local_total * jnp.exp(local_peak - row_peak), pos_value), 'items')  52.7 us
    pmax x1, blocking collectives, body(): row_peak = lax.pmax(local_peak, 'items')  36.2 us
    scatter-add x4, other arithmetic, add_tiles(): grad_tiles.at[cluster_ids.reshape(-1)]  25.8 us
    dot_general x8, matrix products, scores_of(): jnp.einsum('gud,gkcd->gukc', user_rows, picked, preferred_element_type=jn...  17.9 us
  transfers between devices with their start and end apart: 3, of which 2 were waited for; matrix products, arithmetic and copies ran while one was open for 2% of the time, Pallas kernels for 0%

commit v1 on v0

--- a/solution.py
+++ b/solution.py
@@ -121,7 +121,7 @@
     part_weight = lax.dot_general(
         shard_feats.astype(jnp.float32), grad_items, contract, precision=lax.Precision.HIGHEST
     )
-    weight_grad = lax.psum(part_weight, ("users", "items"))
+    weight_grad = lax.psum(lax.psum(part_weight, "users"), "items")
     return (user_loss, user_grad, weight_grad)
 
 

time: 831 us -> 639 us (0.77)
  the two profiles are of different devices: /device:TPU:4 before, /device:TPU:2 now
where the time goes in v1:
time: 639 us; the launch traced here: 638 us
  waiting for transfers between devices  339 us (53%)
  blocking collectives  152 us (24%)
  other arithmetic  51.7 us (8%)
  matrix products  40.8 us (6%)
  local copies, waits for them, and re-layouts  39.6 us (6%)
  between operations  14.6 us (2%)
    psum x2, waiting for transfers between devices, body(): weight_grad = lax.psum(lax.psum(part_weight, 'users'), 'items')  267 us
    reduce_scatter x1, waiting for transfers between devices, body(): lax.psum_scatter(grad_users, 'items', scatter_dimension=0, tiled=True)  70.5 us
    unnamed x1, blocking collectives  63.2 us
    psum x1, blocking collectives, body(): lax.psum((local_total * jnp.exp(local_peak - row_peak), pos_value), 'items')  52.7 us
    pmax x1, blocking collectives, body(): row_peak = lax.pmax(local_peak, 'items')  36.2 us
    scatter-add x4, other arithmetic, add_tiles(): grad_tiles.at[cluster_ids.reshape(-1)]  25.8 us
    dot_general x8, matrix products, scores_of(): jnp.einsum('gud,gkcd->gukc', user_rows, picked, preferred_element_type=jn...  17.9 us
    scatter-add x1, other arithmetic, body(): grad_items = grad_tiles.reshape(shard_rows, emb_width).at[pos_index].add(...  15.9 us
  transfers between devices with their start and end apart: 4, of which 3 were waited for; matrix products, arithmetic and copies ran while one was open for 3% of the time, Pallas kernels for 0%

profile of v1, /device:TPU:2, one launch (start us, length us, event | category | flops | bytes accessed | tf_op | source)
XLA Modules:
  0.0 638.0 jit_solution(994631719547272196)
XLA Ops:
  11.7 63.2 %all-reduce = bf16[1024]{0:T(1024)(128)(2,1)S(1)} all-reduce(bf16[1024]{0:T(1024)(128)(2,1)S(1)} %dynamic-update-slice), channel_id=1, replica_groups=mesh['users'=32,'items'=16] {'users'}, use_global_device_ids=true, to_apply=%add | all-reduce | flops 1024 | bytes 4096
  75.6 8.6 %gather_fusion.5 = f32[2048]{0:T(1024)S(1)} fusion(f32[1024]{0:T(1024)S(1)} %get-tuple-element.174, s32[2048]{0:T(1024)S(1)} %get-tuple-element.164), kind=kCustom, calls=%fused_computation.5 | custom fusion | bytes 24576 | tf_op jit(solution)/shard_map/gather | solution.py:44
  84.9 2.3 convolution_convert_fusion
  87.3 7.5 %gather_fusion.4 = bf16[2048,256]{1,0:T(8,128)(2,1)S(1)} fusion(bf16[1024,256]{1,0:T(8,128)(2,1)S(1)} %convolution_convert_fusion, s32[2048]{0:T(1024)S(1)} %get-tuple-element.164), kind=kCustom, calls=%fused_computation.4 | custom fusion | bytes 2105344 | tf_op jit(solution)/shard_map/gather | solution.py:41
  95.8 17.9 %while.24 = (s32[]{:T(128)}, f32[4,4,128]{2,1,0:T(4,128)S(1)}, f32[4,4,128]{2,1,0:T(4,128)S(1)}, pred[4,4,8]{2,1,0:T(4,128)(4,1)S(1)}, bf16[4,4,128,256]{3,2,1,0...) while((s32[]{:T(128)}, f32[4,4,128]{2,1,0:T(4,128)S(1)}, ...), condition=%wide.region_6.7_spmd, body=%wide.region_3.6_spmd.sunk | while | flops 272633440 | bytes 15036589 | solution.py:73
  97.1 1.9 fusion.43
  113.6 36.2 %pmax.7 = f32[2048]{0:T(1024)S(1)} all-reduce(f32[2048]{0:T(1024)S(1)} %bitcast.148), channel_id=1, replica_groups=mesh['users'=32,'items'=16] {'items'}, use_global_device_ids=true, to_apply=%region_7.8 | all-reduce | flops 2048 | bytes 16384 | tf_op jit(solution)/shard_map/pmax | solution.py:79
  149.8 52.7 %all-reduce.1 = (f32[2048]{0:T(1024)S(1)}, f32[2048]{0:T(1024)S(1)}) all-reduce(f32[2048]{0:T(1024)S(1)} %exponential_multiply_fusion, f32[2048]{0:T(1024)S(1)} %get-tuple-element.161), channel_id=1, replica_groups=mesh['users'=32,'items'=16] {'items'}, use_global_device_ids=true, to_apply=%region_8.9 | all-reduce | flops 4096 | bytes 32768 | tf_op jit(solution)/shard_map/psum | solution.py:80
  202.6 64.0 %while.25 = (s32[]{:T(128)}, f32[8,128,256]{2,1,0:T(8,128)S(1)}, f32[4,4,128,256]{3,2,1,0:T(8,128)}, s32[4,4,8]{2,1,0:T(4,128)S(1)}, pred[4,4,8]{2,1,0:T(4,128)(...) while((s32[]{:T(128)}, f32[8,128,256]{2,1,0:T(8,128)S(1)}, ...), condition=%wide.region_12.13_spmd, body=%wide.region_10.12_spmd.sunk | while | flops 810026176 | bytes 42005372 | solution.py:112
  203.4 2.0 gather_fusion.2
  205.5 2.6 select_convert_fusion.2
  209.4 2.8 convolution_select_fusion.2
  212.1 6.5 %scatter_fusion = f32[8,128,256]{2,1,0:T(8,128)S(1)} fusion(f32[8,128,256]{2,1,0:T(8,128)S(1)} %get-tuple-element.347, s32[32]{0:T(128)S(1)} %fusion.51, f32[32,128,256]{2,1,0:T(8,128)} %bitcast.129), kind=kCustom, calls=%fused_computation.6.clone.1 | custom fusion | flops 1048576 | bytes 12583040 | tf_op jit(solution)/shard_map/while/body/eval_jaxpr/scatter-add | solution.py:99
  219.5 2.0 gather_fusion.2
  221.5 2.6 select_convert_fusion.2
  225.4 2.8 convolution_select_fusion.2
  228.2 6.5 %scatter_fusion = f32[8,128,256]{2,1,0:T(8,128)S(1)} fusion(f32[8,128,256]{2,1,0:T(8,128)S(1)} %get-tuple-element.347, s32[32]{0:T(128)S(1)} %fusion.51, f32[32,128,256]{2,1,0:T(8,128)} %bitcast.129), kind=kCustom, calls=%fused_computation.6.clone.1 | custom fusion | flops 1048576 | bytes 12583040 | tf_op jit(solution)/shard_map/while/body/eval_jaxpr/scatter-add | solution.py:99
  235.5 2.0 gather_fusion.2
  237.5 2.6 select_convert_fusion.2
  241.4 2.8 convolution_select_fusion.2
  244.2 6.4 %scatter_fusion = f32[8,128,256]{2,1,0:T(8,128)S(1)} fusion(f32[8,128,256]{2,1,0:T(8,128)S(1)} %get-tuple-element.347, s32[32]{0:T(128)S(1)} %fusion.51, f32[32,128,256]{2,1,0:T(8,128)} %bitcast.129), kind=kCustom, calls=%fused_computation.6.clone.1 | custom fusion | flops 1048576 | bytes 12583040 | tf_op jit(solution)/shard_map/while/body/eval_jaxpr/scatter-add | solution.py:99
  251.4 2.0 gather_fusion.2
  253.5 2.6 select_convert_fusion.2
  257.4 2.8 convolution_select_fusion.2
  260.2 6.5 %scatter_fusion = f32[8,128,256]{2,1,0:T(8,128)S(1)} fusion(f32[8,128,256]{2,1,0:T(8,128)S(1)} %get-tuple-element.347, s32[32]{0:T(128)S(1)} %fusion.51, f32[32,128,256]{2,1,0:T(8,128)} %bitcast.129), kind=kCustom, calls=%fused_computation.6.clone.1 | custom fusion | flops 1048576 | bytes 12583040 | tf_op jit(solution)/shard_map/while/body/eval_jaxpr/scatter-add | solution.py:99
  266.6 15.9 %scatter_custom_fusion.1 = f32[1024,256]{1,0:T(8,128)S(1)} fusion(f32[1024,256]{1,0:T(8,128)S(1)} %bitcast.128, s32[2048]{0:T(1024)S(1)} %get-tuple-element.165, bf16[2048,256]{1,0:T(8,128)(2,1)} %bitcast.137, f32[2048]{0:T(1024)S(1)} %get-tuple-element.159), kind=kCustom, calls=%fused_computation.46 | custom fusion | flops 1572864 | bytes 2105344 | tf_op jit(solution)/shard_map/scatter-add | solution.py:118
  282.5 4.4 convolution_bitcast_fusion.1
  287.0 129.7 %all-reduce.5.cloned.1.call-done = f32[1024,256]{0,1:T(8,128)} async-done(((f32[1024,256]{0,1:T(8,128)}), f32[1024,256]{0,1:T(8,128)}) %all-reduce.5.cloned.1.call-update) | async-done | bytes 1048592 | tf_op jit(solution)/shard_map/psum | solution.py:124
  416.8 3.3 fusion.17
  420.7 137.7 %all-reduce.7.cloned.1.call-done = f32[1024,256]{0,1:T(8,128)} async-done(((f32[1024,256]{0,1:T(8,128)}), f32[1024,256]{0,1:T(8,128)}) %all-reduce.7.cloned.1.call-update) | async-done | bytes 1048592 | tf_op jit(solution)/shard_map/psum | solution.py:124
  558.4 2.5 copy.14
  561.0 70.5 %reduce-scatter.2.cloned.1.call-done = f32[128,256]{1,0:T(8,128)} async-done(((f32[2048,256]{1,0:T(8,128)}), f32[128,256]{1,0:T(8,128)}) %reduce-scatter.2.cloned.1.call-update) | async-done | bytes 131088 | tf_op jit(solution)/shard_map/reduce_scatter | solution.py:114
  (137 shorter events, 31.3 us)
Async XLA Ops:
  7.2 77.8 %copy-start = (bf16[1024,256]{1,0:T(8,128)(2,1)S(1)}, bf16[1024,256]{1,0:T(8,128)(2,1)}, u32[]{:S(2)}) copy-start(bf16[1024,256]{1,0:T(8,128)(2,1)} %param.14) | copy-start | bytes 1572868
  7.2 77.7 %all-gather.2.cloned.1.call-start = ((), (), s32[]{:S(2)}) async-start(), calls=%async_computation.1 | async-start | bytes 2162688 | tf_op jit(solution)/shard_map/all_gather | solution.py:19
  7.9 408.8 %all-reduce.5.cloned.1.call-start = ((), (), s32[]{:S(2)}) async-start(), calls=%async_computation.3 | async-start | bytes 2097152 | tf_op jit(solution)/shard_map/psum | solution.py:124
  87.2 7.5 %copy-start.2 = (bf16[2048,256]{1,0:T(8,128)(2,1)S(1)}, bf16[2048,256]{1,0:T(8,128)(2,1)}, u32[]{:S(2)}) copy-start(bf16[2048,256]{1,0:T(8,128)(2,1)} %param.10) | copy-start | bytes 3145732
  94.8 1.0 copy-start.5
  94.8 0.7 copy-start.7
  99.0 1.2 copy-start.3
  103.5 1.2 copy-start.3
  107.9 1.2 copy-start.3
  112.4 1.2 copy-start.3
  203.4 2.0 copy-start.4
  205.5 2.6 copy-start.1
  219.4 2.0 copy-start.4
  221.5 2.6 copy-start.1
  235.5 2.0 copy-start.4
  237.5 2.6 copy-start.1
  251.4 2.0 copy-start.4
  253.5 2.6 copy-start.1
  287.0 129.8 %copy-start.6 = (bf16[2048,256]{1,0:T(8,128)(2,1)S(1)}, bf16[2048,256]{1,0:T(8,128)(2,1)}, u32[]{:S(2)}) copy-start(bf16[2048,256]{1,0:T(8,128)(2,1)} %copy-done.5) | copy-start | bytes 3145732
  287.0 271.4 %all-reduce.7.cloned.1.call-start = ((), (), s32[]{:S(2)}) async-start(), calls=%async_computation.4 | async-start | bytes 2097152 | tf_op jit(solution)/shard_map/psum | solution.py:124
  416.8 214.7 %reduce-scatter.2.cloned.1.call-start = ((), (), s32[]{:S(2)}) async-start(), calls=%async_computation.2 | async-start | bytes 2228224 | tf_op jit(solution)/shard_map/reduce_scatter | solution.py:114
Sparse Core Ops, SparseCore 0:
  11.1 63.1 all-gather.1
  287.1 129.5 all-reduce.4
  419.2 139.2 all-reduce.6
  561.7 69.7 reduce-scatter.1
